TPU v7x, 32 devices: a whole 2x2x4 slice. The times are simulated.
32 devices in a mesh: frame: 8 (over z, y), space: 4 (over x, core).
Axes of the slice: x: 2, y: 2, z: 4, core: 2. Of those that a mesh axis runs over, the one named last changes fastest.
Arguments:
- features: bfloat16 [8, 64, 64, 128], P('frame', None, 'space'), may hold values from -6 to 6
- enc_w: bfloat16 [3, 3, 64, 64], replicated, may hold values from -0.25 to 0.25
- enc_b: float32 [64], replicated, may hold values from -3 to 3
- mix_w: bfloat16 [128, 512], replicated, may hold values from -0.25 to 0.25
- mix_b: float32 [128], replicated, may hold values from -3 to 3
- branch3: bfloat16 [3, 3, 512, 16], P(None, None, 'frame'), may hold values from -0.5 to 0.5
- branch5: bfloat16 [5, 5, 512, 16], P(None, None, 'frame'), may hold values from -0.3125 to 0.3125
- branch7: bfloat16 [7, 7, 512, 16], P(None, None, 'frame'), may hold values from -0.21875 to 0.21875
- branch11: bfloat16 [11, 11, 512, 16], P(None, None, 'frame'), may hold values from -0.125 to 0.125
- branch_b: float32 [4, 512], P(None, 'frame'), may hold values from -3 to 3
- dec_w: bfloat16 [3, 3, 64, 64], replicated, may hold values from -0.25 to 0.25
- dec_b: float32 [64], replicated, may hold values from -3 to 3
Outputs:
- decoded: bfloat16 [8, 64, 64, 128], P('frame', None, 'space')
All inputs are finite; a program needn't handle non-finite values.
Results may differ from a plain program's by a relative error of at most 0.019.
Values may be sent and summed in bfloat16 or wider, within the bound.
A program may use at most 64 MiB of HBM per device.

v0:
```python
import jax
import jax.numpy as jnp
from jax import lax
from jax.sharding import PartitionSpec as P

GROUPS = 8


def padded_2(block, sides, width):
    for axis, dim in sides:
        count = lax.axis_size(axis)
        forward = [(i, i + 1) for i in range(count - 1)]
        backward = [(target, source) for source, target in forward]
        low = lax.ppermute(
            lax.slice_in_dim(block, block.shape[dim] - width, None, axis=dim), axis, forward
        )
        high = lax.ppermute(lax.slice_in_dim(block, 0, width, axis=dim), axis, backward)
        block = jnp.concatenate([low, block, high], axis=dim)
    return block


def sweep(padded, weight, kernel_size, start, row_count, col_count):
    summed = jnp.zeros((padded.shape[0], weight.shape[3], row_count, col_count), jnp.float32)
    for row_tap in range(kernel_size):
        band = lax.slice_in_dim(padded, start + row_tap, start + row_tap + row_count, axis=2)
        window = jnp.stack(
            [
                lax.slice_in_dim(band, start + col_tap, start + col_tap + col_count, axis=3)
                for col_tap in range(kernel_size)
            ],
            axis=2,
        )
        summed = summed + jnp.einsum(
            "dgoi,gidrw->gorw", weight[row_tap], window, preferred_element_type=jnp.float32
        )
    return summed


def finish(padded, weight, bias, row_count, col_count):
    padded = jnp.pad(padded, ((0, 0), (0, 0), (0, 0), (1, 1)))
    summed = sweep(padded, weight[:, :, None], 3, 0, row_count, col_count)
    return jax.nn.silu(summed + bias[None, :, None, None]).astype(jnp.bfloat16)


def per_device(
    features,
    enc_w,
    enc_b,
    mix_w,
    mix_b,
    branch3,
    branch5,
    branch7,
    branch11,
    branch_b,
    dec_w,
    dec_b,
):
    frame_index = lax.axis_index("frame")
    frames = lax.axis_size("frame")
    channels, row_count, col_count = (features.shape[1], features.shape[2], features.shape[3])
    padded = padded_2(features, (("space", 2),), 1)
    encoded = finish(padded, enc_w, enc_b, row_count, col_count)
    hidden_count = mix_w.shape[0]
    frame_weight = lax.dynamic_slice_in_dim(mix_w, frame_index * channels, channels, 1)
    partial_mix = jnp.einsum(
        "ji,irw->jrw", frame_weight, encoded[0], preferred_element_type=jnp.float32
    )
    mixed_hidden = (
        lax.psum(partial_mix.astype(jnp.bfloat16), "frame").astype(jnp.float32)
        + mix_b[:, None, None]
    ).astype(jnp.bfloat16)
    per_group = frames * channels // GROUPS
    group_width = hidden_count // GROUPS
    local_groups = max(1, channels // per_group)
    first_group = frame_index * channels // per_group
    own_groups = lax.dynamic_slice_in_dim(
        mixed_hidden, first_group * group_width, local_groups * group_width, 0
    )
    margin = padded_2(own_groups, (("space", 1),), 5)
    margin = jnp.pad(margin, ((0, 0), (0, 0), (5, 5)))
    group_block = margin.reshape(local_groups, group_width, row_count + 10, col_count + 10)
    summed = jnp.zeros((channels, row_count, col_count), jnp.float32)
    for branch_index, weight in enumerate((branch3, branch5, branch7, branch11)):
        kernel_size = weight.shape[0]
        shaped = weight.reshape(
            kernel_size, kernel_size, local_groups, channels // local_groups, group_width
        )
        branch = sweep(group_block, shaped, kernel_size, 5 - kernel_size // 2, row_count, col_count)
        branch = (
            branch.reshape(channels, row_count, col_count) + branch_b[branch_index][:, None, None]
        )
        summed = summed + jnp.where(branch > 0, branch, 0.2 * branch)
    joined = (summed + encoded[0].astype(jnp.float32)).astype(jnp.bfloat16)[None]
    padded_dec = padded_2(joined, (("space", 2),), 1)
    return finish(padded_dec, dec_w, dec_b, row_count, col_count)


def solution(mesh):
    placed = (
        P("frame", None, "space", None),
        P(),
        P(),
        P(),
        P(),
        P(None, None, "frame", None),
        P(None, None, "frame", None),
        P(None, None, "frame", None),
        P(None, None, "frame", None),
        P(None, "frame"),
        P(),
        P(),
    )
    return jax.shard_map(
        per_device,
        mesh=mesh,
        in_specs=placed,
        out_specs=P("frame", None, "space", None),
        check_vma=False,
    )
```

profile of v0, /device:TPU:13, one launch (start us, length us, event | category | flops | bytes accessed | tf_op | source)
XLA Modules:
  0.0 138.5 jit_solution(6459481347505853357)
XLA Ops:
  6.5 1.1 copy.119
  7.6 3.7 %collective-permute-start = (bf16[1,64,1,128]{3,1,2,0:T(8,128)(2,1)S(1)}, bf16[1,64,1,128]{3,1,2,0:T(8,128)(2,1)S(1)}, u32[]{:S(2)}, u32[]{:S(2)}) collective-permute-start(bf16[1,64,1,128]{3,1,2,0:T(8,128)(2,1)S(1)} %get-tuple-element.25), channel_id=1, source_target_pairs={{0,1},{1,2},{2,3},{4,5},{5,6},{6,7},{8,9},{9,10},{10,11},{12,13},{... | collective-permute-start | bytes 49160 | tf_op jit(solution)/shard_map/ppermute | solution.py:14
  11.3 1.9 %collective-permute-start.1 = (bf16[1,64,1,128]{3,1,2,0:T(8,128)(2,1)S(1)}, bf16[1,64,1,128]{3,1,2,0:T(8,128)(2,1)S(1)}, u32[]{:S(2)}, u32[]{:S(2)}) collective-permute-start(bf16[1,64,1,128]{3,1,2,0:T(8,128)(2,1)S(1)} %get-tuple-element.26), channel_id=1, source_target_pairs={{1,0},{2,1},{3,2},{5,4},{6,5},{7,6},{9,8},{10,9},{11,10},{13,12},{... | collective-permute-start | bytes 49160 | tf_op jit(solution)/shard_map/ppermute | solution.py:17
  13.2 3.1 %collective-permute-done.1 = bf16[1,64,1,128]{3,1,2,0:T(8,128)(2,1)S(1)} collective-permute-done((bf16[1,64,1,128]{3,1,2,0:T(8,128)(2,1)S(1)}, bf16[1,64,1,128]{3,1,2,0:T(8,128)(2,1)S(1)}, u32[]{:S(2)}, u32[]{:S(2)}) %collective-permute-start.1) | collective-permute-done | bytes 16416 | tf_op jit(solution)/shard_map/ppermute | solution.py:17
  16.4 0.3 fusion.83
  16.6 0.3 fusion.101
  17.0 0.6 copy-done.6
  17.5 0.3 convolution_bitcast_fusion.3
  17.9 0.3 convolution_bitcast_fusion.4
  18.2 0.3 copy-done.8
  18.5 0.4 multiply_convert_fusion.1
  18.9 1.2 convolution_convert_fusion
  20.2 70.1 %all-reduce.5.cloned.1.call-done = bf16[128,16,128]{2,0,1:T(8,128)(2,1)} async-done(((bf16[128,16,128]{2,0,1:T(8,128)(2,1)}), bf16[128,16,128]{2,0,1:T(8,128)(2,1)}) %all-reduce.5.cloned.1.call-update) | async-done | bytes 524304 | tf_op jit(solution)/shard_map/psum | solution.py:70
  90.3 0.9 add_convert_fusion
  91.3 5.2 %collective-permute-start.2 = (bf16[16,5,128]{2,0,1:T(8,128)(2,1)S(1)}, bf16[16,5,128]{2,0,1:T(8,128)(2,1)S(1)}, u32[]{:S(2)}, u32[]{:S(2)}) collective-permute-start(bf16[16,5,128]{2,0,1:T(8,128)(2,1)S(1)} %get-tuple-element.218), channel_id=1, source_target_pairs={{0,1},{1,2},{2,3},{4,5},{5,6},{6,7},{8,9},{9,10},{10,11},{12,13},{... | collective-permute-start | bytes 61448 | tf_op jit(solution)/shard_map/ppermute | solution.py:14
  96.4 1.9 %collective-permute-start.3 = (bf16[16,5,128]{2,0,1:T(8,128)(2,1)S(1)}, bf16[16,5,128]{2,0,1:T(8,128)(2,1)S(1)}, u32[]{:S(2)}, u32[]{:S(2)}) collective-permute-start(bf16[16,5,128]{2,0,1:T(8,128)(2,1)S(1)} %get-tuple-element.219), channel_id=1, source_target_pairs={{1,0},{2,1},{3,2},{5,4},{6,5},{7,6},{9,8},{10,9},{11,10},{13,12},{... | collective-permute-start | bytes 61448 | tf_op jit(solution)/shard_map/ppermute | solution.py:17
  98.4 3.1 %collective-permute-done.3 = bf16[16,5,128]{2,0,1:T(8,128)(2,1)S(1)} collective-permute-done((bf16[16,5,128]{2,0,1:T(8,128)(2,1)S(1)}, bf16[16,5,128]{2,0,1:T(8,128)(2,1)S(1)}, u32[]{:S(2)}, u32[]{:S(2)}) %collective-permute-start.3) | collective-permute-done | bytes 20512 | tf_op jit(solution)/shard_map/ppermute | solution.py:17
  102.7 0.3 constant_dynamic-update-slice_fusion.80
  103.4 0.4 constant_dynamic-update-slice_fusion.79
  104.5 0.4 constant_dynamic-update-slice_fusion.78
  105.8 0.3 constant_dynamic-update-slice_fusion.77
  106.1 0.3 constant_dynamic-update-slice_fusion.76
  108.2 0.3 constant_dynamic-update-slice_fusion.75
  109.4 0.3 constant_dynamic-update-slice_fusion.74
  111.1 0.4 copy-done.3
  111.5 0.3 convolution_bitcast_fusion.27
  111.7 0.3 convolution_bitcast_fusion.24
  112.0 0.3 convolution_bitcast_fusion.25
  112.3 0.3 convolution_bitcast_fusion.26
  112.6 0.4 copy-done.2
  112.9 0.3 convolution_bitcast_fusion.17
  113.2 0.3 convolution_bitcast_fusion.18
  113.5 0.3 convolution_bitcast_fusion.19
  113.8 0.3 convolution_bitcast_fusion.20
  114.0 0.3 convolution_bitcast_fusion.21
  114.3 0.3 convolution_bitcast_fusion.22
  114.6 0.8 copy-done.1
  115.4 0.3 convolution_bitcast_fusion.13
  115.7 0.3 convolution_bitcast_fusion.14
  116.0 0.3 convolution_bitcast_fusion.15
  116.3 0.3 convolution_bitcast_fusion.10
  116.5 0.3 convolution_bitcast_fusion.11
  116.8 0.3 convolution_bitcast_fusion.12
  117.1 0.3 convolution_bitcast_fusion.6
  117.4 0.3 convolution_bitcast_fusion.7
  117.7 0.3 convolution_bitcast_fusion.8
  118.0 0.3 convolution_bitcast_fusion.9
  118.3 0.5 copy-done.4
  119.1 0.3 convolution_bitcast_fusion.29
  119.3 0.3 compare_select_fusion.3
  119.7 0.4 fusion.67
  120.0 0.5 fusion.66
  120.5 0.6 fusion.65
  121.2 1.9 %collective-permute-start.4 = (bf16[1,64,1,128]{3,1,2,0:T(8,128)(2,1)S(1)}, bf16[1,64,1,128]{3,1,2,0:T(8,128)(2,1)S(1)}, u32[]{:S(2)}, u32[]{:S(2)}) collective-permute-start(bf16[1,64,1,128]{3,1,2,0:T(8,128)(2,1)S(1)} %get-tuple-element.19), channel_id=1, source_target_pairs={{0,1},{1,2},{2,3},{4,5},{5,6},{6,7},{8,9},{9,10},{10,11},{12,13},{... | collective-permute-start | bytes 49160 | tf_op jit(solution)/shard_map/ppermute | solution.py:14
  123.1 2.4 %collective-permute-start.5 = (bf16[1,64,1,128]{3,1,2,0:T(8,128)(2,1)S(1)}, bf16[1,64,1,128]{3,1,2,0:T(8,128)(2,1)S(1)}, u32[]{:S(2)}, u32[]{:S(2)}) collective-permute-start(bf16[1,64,1,128]{3,1,2,0:T(8,128)(2,1)S(1)} %get-tuple-element.20), channel_id=1, source_target_pairs={{1,0},{2,1},{3,2},{5,4},{6,5},{7,6},{9,8},{10,9},{11,10},{13,12},{... | collective-permute-start | bytes 49160 | tf_op jit(solution)/shard_map/ppermute | solution.py:17
  125.5 2.6 %collective-permute-done.5 = bf16[1,64,1,128]{3,1,2,0:T(8,128)(2,1)S(1)} collective-permute-done((bf16[1,64,1,128]{3,1,2,0:T(8,128)(2,1)S(1)}, bf16[1,64,1,128]{3,1,2,0:T(8,128)(2,1)S(1)}, u32[]{:S(2)}, u32[]{:S(2)}) %collective-permute-start.5) | collective-permute-done | bytes 16416 | tf_op jit(solution)/shard_map/ppermute | solution.py:17
  128.2 0.3 select_maximum_fusion
  128.5 0.4 slice_bitcast_fusion.5
  128.9 0.5 copy-done.7
  129.4 0.3 convolution_bitcast_fusion.1
  129.7 0.3 convolution_bitcast_fusion
  130.0 0.3 copy-done.10
  130.4 0.4 fusion.84
  130.7 0.9 copy.52
  (74 shorter events, 7.3 us)
Async XLA Ops:
  6.5 12.4 %copy-start = (bf16[128,512]{1,0:T(8,128)(2,1)S(1)}, bf16[128,512]{1,0:T(8,128)(2,1)}, u32[]{:S(2)}) copy-start(bf16[128,512]{1,0:T(8,128)(2,1)} %param.15) | copy-start | bytes 393220
  6.5 83.8 %all-reduce.5.cloned.1.call-start = ((), (), s32[]{:S(2)}) async-start(), calls=%async_computation | async-start | bytes 1048576 | tf_op jit(solution)/shard_map/psum | solution.py:70
  7.6 5.6 %collective-permute-start = (bf16[1,64,1,128]{3,1,2,0:T(8,128)(2,1)S(1)}, bf16[1,64,1,128]{3,1,2,0:T(8,128)(2,1)S(1)}, u32[]{:S(2)}, u32[]{:S(2)}) collective-permute-start(bf16[1,64,1,128]{3,1,2,0:T(8,128)(2,1)S(1)} %get-tuple-element.25), channel_id=1, source_target_pairs={{0,1},{1,2},{2,3},{4,5},{5,6},{6,7},{8,9},{9,10},{10,11},{12,13},{... | collective-permute-start | bytes 49160 | tf_op jit(solution)/shard_map/ppermute | solution.py:14
  11.3 5.1 %collective-permute-start.1 = (bf16[1,64,1,128]{3,1,2,0:T(8,128)(2,1)S(1)}, bf16[1,64,1,128]{3,1,2,0:T(8,128)(2,1)S(1)}, u32[]{:S(2)}, u32[]{:S(2)}) collective-permute-start(bf16[1,64,1,128]{3,1,2,0:T(8,128)(2,1)S(1)} %get-tuple-element.26), channel_id=1, source_target_pairs={{1,0},{2,1},{3,2},{5,4},{6,5},{7,6},{9,8},{10,9},{11,10},{13,12},{... | collective-permute-start | bytes 49160 | tf_op jit(solution)/shard_map/ppermute | solution.py:17
  16.6 0.9 copy-start.6
  17.9 0.7 copy-start.8
  18.9 1.2 copy-start.9
  18.9 79.5 %copy-start.5 = (f32[4,64]{1,0:T(4,128)S(1)}, f32[4,64]{1,0:T(4,128)}, u32[]{:S(2)}) copy-start(f32[4,64]{1,0:T(4,128)} %param.21) | copy-start | bytes 3076
  91.3 7.1 %collective-permute-start.2 = (bf16[16,5,128]{2,0,1:T(8,128)(2,1)S(1)}, bf16[16,5,128]{2,0,1:T(8,128)(2,1)S(1)}, u32[]{:S(2)}, u32[]{:S(2)}) collective-permute-start(bf16[16,5,128]{2,0,1:T(8,128)(2,1)S(1)} %get-tuple-element.218), channel_id=1, source_target_pairs={{0,1},{1,2},{2,3},{4,5},{5,6},{6,7},{8,9},{9,10},{10,11},{12,13},{... | collective-permute-start | bytes 61448 | tf_op jit(solution)/shard_map/ppermute | solution.py:14
  96.4 5.1 %collective-permute-start.3 = (bf16[16,5,128]{2,0,1:T(8,128)(2,1)S(1)}, bf16[16,5,128]{2,0,1:T(8,128)(2,1)S(1)}, u32[]{:S(2)}, u32[]{:S(2)}) collective-permute-start(bf16[16,5,128]{2,0,1:T(8,128)(2,1)S(1)} %get-tuple-element.219), channel_id=1, source_target_pairs={{1,0},{2,1},{3,2},{5,4},{6,5},{7,6},{9,8},{10,9},{11,10},{13,12},{... | collective-permute-start | bytes 61448 | tf_op jit(solution)/shard_map/ppermute | solution.py:17
  110.6 0.9 copy-start.3
  112.0 0.9 copy-start.2
  114.3 1.0 copy-start.1
  118.0 0.8 copy-start.4
  121.2 4.3 %collective-permute-start.4 = (bf16[1,64,1,128]{3,1,2,0:T(8,128)(2,1)S(1)}, bf16[1,64,1,128]{3,1,2,0:T(8,128)(2,1)S(1)}, u32[]{:S(2)}, u32[]{:S(2)}) collective-permute-start(bf16[1,64,1,128]{3,1,2,0:T(8,128)(2,1)S(1)} %get-tuple-element.19), channel_id=1, source_target_pairs={{0,1},{1,2},{2,3},{4,5},{5,6},{6,7},{8,9},{9,10},{10,11},{12,13},{... | collective-permute-start | bytes 49160 | tf_op jit(solution)/shard_map/ppermute | solution.py:14
  123.1 5.1 %collective-permute-start.5 = (bf16[1,64,1,128]{3,1,2,0:T(8,128)(2,1)S(1)}, bf16[1,64,1,128]{3,1,2,0:T(8,128)(2,1)S(1)}, u32[]{:S(2)}, u32[]{:S(2)}) collective-permute-start(bf16[1,64,1,128]{3,1,2,0:T(8,128)(2,1)S(1)} %get-tuple-element.20), channel_id=1, source_target_pairs={{1,0},{2,1},{3,2},{5,4},{6,5},{7,6},{9,8},{10,9},{11,10},{13,12},{... | collective-permute-start | bytes 49160 | tf_op jit(solution)/shard_map/ppermute | solution.py:17
  128.4 0.9 copy-start.7
  129.7 0.7 copy-start.10
Sparse Core Ops, SparseCore 0:
  20.2 70.0 all-reduce.4
where the time goes:
time: 140 us; the launch traced here: 138 us
  waiting for transfers between devices  79 us (56%)
  starting transfers between devices  17 us (12%)
  local copies, waits for them, and re-layouts  15.2 us (11%)
  between operations  14.2 us (10%)
  matrix products  11 us (8%)
  other arithmetic  1.95 us (1%)
    psum x1, waiting for transfers between devices, per_device(): lax.psum(partial_mix.astype(jnp.bfloat16), 'frame').astype(jnp.float32)  70.1 us
    unnamed x74, local copies, waits for them, and re-layouts  13.1 us
    ppermute x3, starting transfers between devices, padded_2(): lax.ppermute(lax.slice_in_dim(block, block.shape[dim] - width, None, axis...  10.8 us
    dot_general x32, matrix products, sweep(): jnp.einsum('dgoi,gidrw->gorw', weight[row_tap], window, preferred_element...  9.89 us
    ppermute x3, waiting for transfers between devices, padded_2(): lax.ppermute(lax.slice_in_dim(block, 0, width, axis=dim), axis, backward)  8.89 us
    ppermute x3, starting transfers between devices, padded_2(): lax.ppermute(lax.slice_in_dim(block, 0, width, axis=dim), axis, backward)  6.24 us
  transfers between devices with their start and end apart: 7, of which 4 were waited for; matrix products, arithmetic and copies ran while one was open for 0% of the time, Pallas kernels for 0%

commit v1 on v0

v1 whole, which is shorter than its diff:
```python
import functools

import jax
import jax.numpy as jnp
from jax import lax
from jax.experimental import pallas as pl
from jax.experimental.pallas import tpu as pltpu
from jax.sharding import PartitionSpec as P

GROUPS = 8
SIZES = (3, 5, 7, 11)
BIG = 11
PAD = BIG // 2
BF16 = jnp.bfloat16
F32 = jnp.float32
MESH = pl.DeviceIdType.MESH


def shifted(x, step):
    if step == 0:
        return x
    width = x.shape[1]
    lane = lax.broadcasted_iota(jnp.int32, x.shape, 1) + step
    rolled = pltpu.roll(x, (-step) % width, 1)
    return jnp.where((lane >= 0) & (lane < width), rolled, 0.0)


def column(row, count, start=0):
    shape = (count, row.shape[1])
    hit = lax.broadcasted_iota(jnp.int32, shape, 1) == (
        lax.broadcasted_iota(jnp.int32, shape, 0) + start
    )
    return jnp.sum(jnp.where(hit, jnp.broadcast_to(row, shape), 0.0), axis=1, keepdims=True)


def silu(v):
    return v / (1.0 + jnp.exp(-v))


def kernel(
    frames,
    spaces,
    feat,
    enc_w,
    enc_b,
    mix_w,
    mix_b,
    branch3,
    branch5,
    branch7,
    branch11,
    branch_b,
    dec_w,
    dec_b,
    out,
    w3e,
    w3d,
    wbig,
    raw3,
    raw5,
    raw7,
    raw11,
    s3,
    s11,
    enc,
    part,
    arrived,
    hid,
    joined,
    x_halo,
    h_halo,
    j_halo,
    load_sem,
    x_send,
    x_recv,
    p_send,
    p_recv,
    h_send,
    h_recv,
    j_send,
    j_recv,
):
    rows, channels, width = feat.shape
    inner = part.shape[2]
    out_channels = frames * channels
    frame, space = lax.axis_index("frame"), lax.axis_index("space")
    above, below = space > 0, space < spaces - 1

    raws = (raw3, raw5, raw7, raw11)
    loads = [
        pltpu.make_async_copy(source, target, load_sem.at[n])
        for n, (source, target) in enumerate(
            zip((branch3, branch5, branch7, branch11), raws)
        )
    ]
    for load in loads:
        load.start()

    barrier = pltpu.get_barrier_semaphore()

    def greet(device):
        pl.semaphore_signal(barrier, inc=1, device_id=device, device_id_type=MESH)

    @pl.when(above)
    def _():
        greet({"space": space - 1})

    @pl.when(below)
    def _():
        greet({"space": space + 1})

    for step in range(1, frames):
        greet({"frame": lax.rem(frame + step, frames)})

    def up(first, halo, send, recv):
        return pltpu.make_async_remote_copy(
            src_ref=first,
            dst_ref=halo.at[1],
            send_sem=send.at[1],
            recv_sem=recv.at[1],
            device_id={"space": space - 1},
            device_id_type=MESH,
        )

    def down(last, halo, send, recv):
        return pltpu.make_async_remote_copy(
            src_ref=last,
            dst_ref=halo.at[0],
            send_sem=send.at[0],
            recv_sem=recv.at[0],
            device_id={"space": space + 1},
            device_id_type=MESH,
        )

    def edges_start(first, last, *rest):
        @pl.when(above)
        def _():
            up(first, *rest).start()

        @pl.when(below)
        def _():
            down(last, *rest).start()

    def edges_sent(first, last, *rest):
        @pl.when(above)
        def _():
            up(first, *rest).wait_send()

        @pl.when(below)
        def _():
            down(last, *rest).wait_send()

    def put3(row, x):
        x = x.astype(F32)
        for tap in range(3):
            s3[row, tap * channels : (tap + 1) * channels, :] = shifted(x, tap - 1).astype(BF16)

    def edges3(first, last, halo, send, recv):
        @pl.when(above)
        def _():
            down(last, halo, send, recv).wait_recv()
            put3(0, halo[0])

        @pl.when(jnp.logical_not(above))
        def _():
            s3[0] = jnp.zeros((3 * channels, width), BF16)

        @pl.when(below)
        def _():
            up(first, halo, send, recv).wait_recv()
            put3(rows + 1, halo[1])

        @pl.when(jnp.logical_not(below))
        def _():
            s3[rows + 1] = jnp.zeros((3 * channels, width), BF16)

    def conv3(weight, bias, row):
        depth = 9 * channels
        window = jnp.concatenate(
            [s3[pl.ds(row + h, 3)].reshape(depth, width) for h in range(2)], axis=1
        )
        return silu(jnp.dot(weight[...], window, preferred_element_type=F32) + bias).astype(BF16)

    def lay3(source, target):
        flat = [source[tap // 3, tap % 3] for tap in range(9)]
        for pair in range(4):
            target[:, pair * 2 * channels : (pair + 1) * 2 * channels] = jnp.concatenate(
                flat[2 * pair : 2 * pair + 2], axis=1
            )
        target[:, 8 * channels :] = flat[8]

    lay3(enc_w, w3e)
    enc_col = column(enc_b[...], channels)

    per_block = 128 // channels
    block = mix_w[:, pl.ds(pl.multiple_of((frame // per_block) * 128, 128), 128)]
    own_mix = block[:, :channels]
    for piece in range(1, per_block):
        own_mix = jnp.where(
            lax.rem(frame, per_block) == piece,
            block[:, piece * channels : (piece + 1) * channels],
            own_mix,
        )

    pl.semaphore_wait(
        barrier, frames - 1 + above.astype(jnp.int32) + below.astype(jnp.int32)
    )

    x_args = (feat.at[0], feat.at[rows - 1], x_halo, x_send, x_recv)
    edges_start(*x_args)

    @pl.loop(0, rows)
    def _(row):
        put3(row + 1, feat[row])

    def encode(row):
        e = conv3(w3e, enc_col, row)
        p = jnp.dot(own_mix, e, preferred_element_type=F32).astype(BF16)
        for h in range(2):
            enc[row + h] = e[:, h * width : (h + 1) * width]
            part[:, row + h] = p[:, h * width : (h + 1) * width].reshape(
                p.shape[0] // inner, inner, width
            )

    @pl.loop(1, rows // 2 - 1)
    def _(pair):
        encode(2 * pair)

    edges3(*x_args)
    encode(0)
    encode(rows - 2)

    per_group = out_channels // GROUPS

    def group_of(index):
        return (index * channels) // per_group

    def share(step):
        peer = lax.rem(frame + step, frames)
        return pltpu.make_async_remote_copy(
            src_ref=part.at[group_of(peer)],
            dst_ref=arrived.at[step - 1],
            send_sem=p_send.at[step - 1],
            recv_sem=p_recv.at[step - 1],
            device_id={"frame": peer},
            device_id_type=MESH,
        )

    for step in range(1, frames):
        share(step).start()

    lay3(dec_w, w3d)
    dec_col = column(dec_b[...], channels)
    branch_col = jnp.concatenate(
        [column(branch_b[n : n + 1, :], channels) for n in range(4)], axis=0
    )
    mix_col = column(mix_b[...], inner, group_of(frame) * inner)
    for load in loads:
        load.wait()
    taps = BIG * BIG
    many = 128 // inner
    empty = jnp.zeros((channels, inner), BF16)
    for n, (size, raw) in enumerate(zip(SIZES, raws)):
        skip = PAD - size // 2
        for first in range(0, taps, many):
            pieces, used = [], False
            for tap in range(first, min(first + many, taps)):
                a, b = tap // BIG - skip, tap % BIG - skip
                inside = 0 <= a < size and 0 <= b < size
                used = used or inside
                pieces.append(raw[a, b] if inside else empty)
            count = len(pieces) * inner
            value = (
                jnp.concatenate(pieces, axis=1) if used else jnp.zeros((channels, count), BF16)
            )
            wbig[n * channels : (n + 1) * channels, first * inner : first * inner + count] = value

    total = part[group_of(frame)].astype(F32)
    for step in range(1, frames):
        share(step).wait_recv()
        total = total + arrived[step - 1].astype(F32)
    total = (total + mix_col[None]).astype(BF16)
    hid[...] = total
    h_args = (hid.at[0:PAD], hid.at[rows - PAD : rows], h_halo, h_send, h_recv)
    edges_start(*h_args)

    def put11(row, x):
        count = x.shape[0]
        x = x.astype(F32).reshape(count * inner, width)
        for tap in range(BIG):
            s11[row : row + count, tap * inner : (tap + 1) * inner, :] = (
                shifted(x, tap - PAD).astype(BF16).reshape(count, inner, width)
            )

    put11(PAD, total)

    def mixed(row):
        depth = BIG * BIG * inner
        window = jnp.concatenate(
            [s11[pl.ds(row + h, BIG)].reshape(depth, width) for h in range(2)], axis=1
        )
        pre = jnp.dot(wbig[...], window, preferred_element_type=F32) + branch_col
        pre = jnp.where(pre > 0, pre, 0.2 * pre)
        pre = pre.reshape(4, channels, 2 * width)
        total = pre[0] + pre[1] + pre[2] + pre[3]
        for h in range(2):
            whole = (total[:, h * width : (h + 1) * width] + enc[row + h].astype(F32)).astype(BF16)
            joined[row + h] = whole
            put3(row + h + 1, whole)

    low = (PAD + 1) // 2
    high = (rows - PAD) // 2

    @pl.loop(low, high)
    def _(pair):
        mixed(2 * pair)

    nothing = jnp.zeros((PAD, BIG * inner, width), BF16)

    @pl.when(above)
    def _():
        down(h_args[1], *h_args[2:]).wait_recv()
        put11(0, h_halo[0])

    @pl.when(jnp.logical_not(above))
    def _():
        s11[0:PAD] = nothing

    @pl.when(below)
    def _():
        up(h_args[0], *h_args[2:]).wait_recv()
        put11(rows + PAD, h_halo[1])

    @pl.when(jnp.logical_not(below))
    def _():
        s11[rows + PAD : rows + 2 * PAD] = nothing

    @pl.loop(0, 2)
    def _(side):
        mixed(side * (rows - 2))

    j_args = (joined.at[0], joined.at[rows - 1], j_halo, j_send, j_recv)
    edges_start(*j_args)

    @pl.loop(1, low)
    def _(pair):
        mixed(2 * pair)

    @pl.loop(high, rows // 2 - 1)
    def _(pair):
        mixed(2 * pair)

    def decode(row):
        d = conv3(w3d, dec_col, row)
        for h in range(2):
            out[row + h] = d[:, h * width : (h + 1) * width]

    @pl.loop(1, rows // 2 - 1)
    def _(pair):
        decode(2 * pair)

    edges3(*j_args)
    decode(0)
    decode(rows - 2)

    edges_sent(*x_args)
    edges_sent(*h_args)
    edges_sent(*j_args)
    for step in range(1, frames):
        share(step).wait_send()


def per_device(
    frames,
    spaces,
    features,
    enc_w,
    enc_b,
    mix_w,
    mix_b,
    branch3,
    branch5,
    branch7,
    branch11,
    branch_b,
    dec_w,
    dec_b,
):
    channels, rows, width = features.shape[1:]
    inner = mix_w.shape[0] // GROUPS
    vmem = pl.BlockSpec(memory_space=pltpu.VMEM)
    hbm = pl.BlockSpec(memory_space=pl.ANY)
    strip = (rows, channels, width)
    pair = pltpu.SemaphoreType.DMA((2,))
    many = pltpu.SemaphoreType.DMA((frames - 1,))
    decoded = pl.pallas_call(
        functools.partial(kernel, frames, spaces),
        out_shape=jax.ShapeDtypeStruct(strip, BF16),
        in_specs=[vmem] * 5 + [hbm] * 4 + [vmem] * 3,
        out_specs=vmem,
        scratch_shapes=[
            pltpu.VMEM((channels, 9 * channels), BF16),
            pltpu.VMEM((channels, 9 * channels), BF16),
            pltpu.VMEM((4 * channels, BIG * BIG * inner), BF16),
            pltpu.VMEM(branch3.shape, BF16),
            pltpu.VMEM(branch5.shape, BF16),
            pltpu.VMEM(branch7.shape, BF16),
            pltpu.VMEM(branch11.shape, BF16),
            pltpu.VMEM((rows + 2, 3 * channels, width), BF16),
            pltpu.VMEM((rows + 2 * PAD, BIG * inner, width), BF16),
            pltpu.VMEM(strip, BF16),
            pltpu.VMEM((GROUPS, rows, inner, width), BF16),
            pltpu.VMEM((frames - 1, rows, inner, width), BF16),
            pltpu.VMEM((rows, inner, width), BF16),
            pltpu.VMEM(strip, BF16),
            pltpu.VMEM((2, channels, width), BF16),
            pltpu.VMEM((2, PAD, inner, width), BF16),
            pltpu.VMEM((2, channels, width), BF16),
            pltpu.SemaphoreType.DMA((4,)),
            pair,
            pair,
            many,
            many,
            pair,
            pair,
            pair,
            pair,
        ],
        compiler_params=pltpu.CompilerParams(
            collective_id=0, has_side_effects=True, vmem_limit_bytes=40 * 2**20
        ),
    )(
        jnp.transpose(features[0], (1, 0, 2)),
        enc_w,
        enc_b[None],
        mix_w,
        mix_b[None],
        branch3,
        branch5,
        branch7,
        branch11,
        branch_b,
        dec_w,
        dec_b[None],
    )
    return jnp.transpose(decoded, (1, 0, 2))[None]


def solution(mesh):
    placed = (
        P("frame", None, "space", None),
        P(),
        P(),
        P(),
        P(),
        P(None, None, "frame", None),
        P(None, None, "frame", None),
        P(None, None, "frame", None),
        P(None, None, "frame", None),
        P(None, "frame"),
        P(),
        P(),
    )
    return jax.shard_map(
        functools.partial(per_device, mesh.shape["frame"], mesh.shape["space"]),
        mesh=mesh,
        in_specs=placed,
        out_specs=P("frame", None, "space", None),
        check_vma=False,
    )
```

time: 140 us -> 41.7 us (0.30)
  waiting for transfers between devices: 79 us -> 0 us
  Pallas kernels: 0 us -> 29.2 us
  starting transfers between devices: 17 us -> 0 us
  between operations: 14.2 us -> 0.1 us
  matrix products: 11 us -> 0 us
  local copies, waits for them, and re-layouts: 15.2 us -> 12.1 us
  other arithmetic: 1.95 us -> 0 us
    psum x1 -> x0, waiting for transfers between devices: 70.1 us -> none  [per_device(): lax.psum(partial_mix.astype(jnp.bfloat16), 'frame').astype(jnp.float32)]
    pallas_call x0 -> x1, Pallas kernels: none -> 29.2 us  [per_device(): pl.pallas_call(functools.partial(kernel, frames, spaces), out_shape=jax.S...]
    ppermute x6 -> x0, starting transfers between devices: 17 us -> none  [the longest x3 10.8 us: padded_2(): lax.ppermute(lax.slice_in_dim(block, block.shape[dim] - width, None, axis...]
    dot_general x33 -> x0, matrix products: 11 us -> none  [the longest x32 9.89 us: sweep(): jnp.einsum('dgoi,gidrw->gorw', weight[row_tap], window, preferred_element...]
    ppermute x6 -> x0, waiting for transfers between devices: 8.9 us -> none  [the longest x3 8.89 us: padded_2(): lax.ppermute(lax.slice_in_dim(block, 0, width, axis=dim), axis, backward)]
    unnamed x74 -> x21, local copies, waits for them, and re-layouts: 13.1 us -> 11.2 us
  transfers between devices with their start and end apart: 7 -> 0, of which waited for: 4 -> 0; matrix products, arithmetic and copies ran while one was open for 0% -> 0% of each run, Pallas kernels for 0% -> 0%
where the time goes in v1:
time: 41.7 us; the launch traced here: 41.4 us
  Pallas kernels  29.2 us (70%)
  local copies, waits for them, and re-layouts  12.1 us (29%)
    pallas_call x1, Pallas kernels, per_device(): pl.pallas_call(functools.partial(kernel, frames, spaces), out_shape=jax.S...  29.2 us
    unnamed x21, local copies, waits for them, and re-layouts  11.2 us
    broadcast_in_dim x1, local copies, waits for them, and re-layouts, per_device(): return jnp.transpose(decoded, (1, 0, 2))[None]  0.88 us

profile of v1, /device:TPU:13, one launch (start us, length us, event | category | flops | bytes accessed | tf_op | source)
XLA Modules:
  0.0 41.4 jit_solution(1510109849120781790)
XLA Ops:
  0.0 1.5 %copy.14.branch3 = bf16[3,3,64,16]{3,2,1,0:T(8,128)(2,1)} copy(bf16[3,3,64,16]{2,3,1,0:T(8,128)(2,1)} %param.17) | data formatting | bytes 36864 | tf_op args[5]
  1.5 1.0 %copy.20 = bf16[1,64,16,128]{3,1,2,0:T(8,128)(2,1)S(1)} copy(bf16[1,64,16,128]{3,2,1,0:T(8,128)(2,1)} %param.12) | data formatting | bytes 524288 | tf_op args[0]
  2.6 0.0 copy-start.4
  2.6 0.0 copy-start.5
  2.6 0.0 copy-start.6
  2.6 0.0 copy-start.7
  2.6 1.1 %copy.15.branch5 = bf16[5,5,64,16]{3,2,1,0:T(8,128)(2,1)S(1)} copy(bf16[5,5,64,16]{2,3,1,0:T(8,128)(2,1)} %param.18) | data formatting | bytes 102400 | tf_op args[6]
  3.8 1.3 %copy.16.branch7 = bf16[7,7,64,16]{3,2,1,0:T(8,128)(2,1)S(1)} copy(bf16[7,7,64,16]{2,3,1,0:T(8,128)(2,1)} %param.19) | data formatting | bytes 200704 | tf_op args[7]
  5.1 2.5 %copy.17.branch11 = bf16[11,11,64,16]{3,2,1,0:T(8,128)(2,1)S(1)} copy(bf16[11,11,64,16]{2,3,1,0:T(8,128)(2,1)} %param.20) | data formatting | bytes 495616 | tf_op args[8]
  7.6 0.0 copy-done.4
  7.6 0.0 copy-done.5
  7.6 0.0 copy-done.6
  7.6 0.0 copy-done.7
  7.6 0.0 copy-start
  7.7 0.9 %copy-done = bf16[3,3,64,16]{3,2,1,0:T(8,128)(2,1)S(1)} copy-done((bf16[3,3,64,16]{3,2,1,0:T(8,128)(2,1)S(1)}, bf16[3,3,64,16]{3,2,1,0:T(8,128)(2,1)}, u32[]{:S(2)}) %copy-start) | copy-done | bytes 18456
  8.6 0.0 copy-start.1
  8.6 0.9 %copy-done.1 = bf16[3,3,64,64]{3,2,1,0:T(8,128)(2,1)S(1)} copy-done((bf16[3,3,64,64]{3,2,1,0:T(8,128)(2,1)S(1)}, bf16[3,3,64,64]{3,2,1,0:T(8,128)(2,1)}, u32[]{:S(2)}) %copy-start.1) | copy-done | bytes 73752
  9.5 0.0 copy-start.2
  9.5 0.9 %copy-done.2 = bf16[3,3,64,64]{3,2,1,0:T(8,128)(2,1)S(1)} copy-done((bf16[3,3,64,64]{3,2,1,0:T(8,128)(2,1)S(1)}, bf16[3,3,64,64]{3,2,1,0:T(8,128)(2,1)}, u32[]{:S(2)}) %copy-start.2) | copy-done | bytes 73752
  10.4 0.0 copy-start.3
  10.4 0.9 %copy-done.3 = bf16[128,512]{1,0:T(8,128)(2,1)S(1)} copy-done((bf16[128,512]{1,0:T(8,128)(2,1)S(1)}, bf16[128,512]{1,0:T(8,128)(2,1)}, u32[]{:S(2)}) %copy-start.3) | copy-done | bytes 131096
  11.3 29.2 %shard_map.118 = bf16[16,64,128]{2,1,0:T(8,128)(2,1)S(1)} custom-call(bf16[16,64,128]{2,1,0:T(8,128)(2,1)S(1)} %bitcast.12, bf16[3,3,64,64]{3,2,1,0:T(8,128)(2,1)S(1)} %copy-done.1, f32[1,64]{1,0:T(1,128)S(1)} %bitcast.13, bf16[128,512]{1,0:T(8,128)(2,1)S(1)} %copy-done.3, f32[1,128]{1,0:T(1,128)S(1)} %bitcast.14, bf16[3,3,64,16]{3,2,1,0:T(8,128)(2,1)S(1)} %copy-done, ...), custom_call_target="tpu_custom_call" | custom-call | tf_op jit(solution)/shard_map/pallas_call | solution.py:396
  40.5 0.9 %copy.18 = bf16[1,64,16,128]{3,2,1,0:T(8,128)(2,1)} copy(bf16[1,64,16,128]{3,1,2,0:T(8,128)(2,1)S(1)} %bitcast.11) | data formatting | bytes 524288 | tf_op jit(solution)/shard_map/broadcast_in_dim | solution.py:446
Async XLA Ops:
  2.6 5.0 %copy-start.4 = (f32[4,64]{1,0:T(4,128)S(1)}, f32[4,64]{1,0:T(4,128)}, u32[]{:S(2)}) copy-start(f32[4,64]{1,0:T(4,128)} %branch_b.1) | copy-start | bytes 3076
  2.6 5.0 %copy-start.5 = (f32[64]{0:T(128)S(1)}, f32[64]{0:T(128)}, u32[]{:S(2)}) copy-start(f32[64]{0:T(128)} %param.14) | copy-start | bytes 772
  2.6 5.0 %copy-start.6 = (f32[128]{0:T(128)S(1)}, f32[128]{0:T(128)}, u32[]{:S(2)}) copy-start(f32[128]{0:T(128)} %param.16) | copy-start | bytes 1540
  2.6 5.0 %copy-start.7 = (f32[64]{0:T(128)S(1)}, f32[64]{0:T(128)}, u32[]{:S(2)}) copy-start(f32[64]{0:T(128)} %param.23) | copy-start | bytes 772
  7.6 0.9 %copy-start = (bf16[3,3,64,16]{3,2,1,0:T(8,128)(2,1)S(1)}, bf16[3,3,64,16]{3,2,1,0:T(8,128)(2,1)}, u32[]{:S(2)}) copy-start(bf16[3,3,64,16]{3,2,1,0:T(8,128)(2,1)} %copy.14.branch3) | copy-start | bytes 55300
  8.6 0.9 %copy-start.1 = (bf16[3,3,64,64]{3,2,1,0:T(8,128)(2,1)S(1)}, bf16[3,3,64,64]{3,2,1,0:T(8,128)(2,1)}, u32[]{:S(2)}) copy-start(bf16[3,3,64,64]{3,2,1,0:T(8,128)(2,1)} %enc_w.1) | copy-start | bytes 221188
  9.5 0.9 %copy-start.2 = (bf16[3,3,64,64]{3,2,1,0:T(8,128)(2,1)S(1)}, bf16[3,3,64,64]{3,2,1,0:T(8,128)(2,1)}, u32[]{:S(2)}) copy-start(bf16[3,3,64,64]{3,2,1,0:T(8,128)(2,1)} %dec_w.1) | copy-start | bytes 221188
  10.4 0.9 %copy-start.3 = (bf16[128,512]{1,0:T(8,128)(2,1)S(1)}, bf16[128,512]{1,0:T(8,128)(2,1)}, u32[]{:S(2)}) copy-start(bf16[128,512]{1,0:T(8,128)(2,1)} %mix_w.1) | copy-start | bytes 393220

commit v2 on v1

--- a/solution.py
+++ b/solution.py
@@ -40,19 +40,25 @@
 def kernel(
     frames,
     spaces,
-    feat,
-    enc_w,
-    enc_b,
+    features,
+    enc_w_all,
     mix_w,
-    mix_b,
     branch3,
     branch5,
     branch7,
     branch11,
+    dec_w_all,
+    enc_b,
+    mix_b,
     branch_b,
-    dec_w,
     dec_b,
     out,
+    planes,
+    feat,
+    enc_w,
+    mix_block,
+    dec_w,
+    wt,
     w3e,
     w3d,
     wbig,
@@ -86,11 +92,22 @@
     frame, space = lax.axis_index("frame"), lax.axis_index("space")
     above, below = space > 0, space < spaces - 1
 
+    per_block = 128 // channels
+    mix_columns = pl.ds(pl.multiple_of((frame // per_block) * 128, 128), 128)
     raws = (raw3, raw5, raw7, raw11)
     loads = [
         pltpu.make_async_copy(source, target, load_sem.at[n])
         for n, (source, target) in enumerate(
-            zip((branch3, branch5, branch7, branch11), raws)
+            (
+                (features.at[0], planes),
+                (enc_w_all, enc_w),
+                (mix_w.at[:, mix_columns], mix_block),
+                (dec_w_all, dec_w),
+                (branch3, raw3),
+                (branch5, raw5),
+                (branch7, raw7),
+                (branch11, raw11),
+            )
         )
     ]
     for load in loads:
@@ -189,11 +206,13 @@
             )
         target[:, 8 * channels :] = flat[8]
 
+    loads[0].wait()
+    feat[...] = jnp.transpose(planes[...], (1, 0, 2))
+    enc_col = column(enc_b[...], channels)
+    loads[1].wait()
     lay3(enc_w, w3e)
-    enc_col = column(enc_b[...], channels)
-
-    per_block = 128 // channels
-    block = mix_w[:, pl.ds(pl.multiple_of((frame // per_block) * 128, 128), 128)]
+    loads[2].wait()
+    block = mix_block[...]
     own_mix = block[:, :channels]
     for piece in range(1, per_block):
         own_mix = jnp.where(
@@ -249,31 +268,29 @@
     for step in range(1, frames):
         share(step).start()
 
-    lay3(dec_w, w3d)
     dec_col = column(dec_b[...], channels)
     branch_col = jnp.concatenate(
         [column(branch_b[n : n + 1, :], channels) for n in range(4)], axis=0
     )
     mix_col = column(mix_b[...], inner, group_of(frame) * inner)
-    for load in loads:
+    for load in loads[3:]:
         load.wait()
-    taps = BIG * BIG
-    many = 128 // inner
-    empty = jnp.zeros((channels, inner), BF16)
-    for n, (size, raw) in enumerate(zip(SIZES, raws)):
-        skip = PAD - size // 2
-        for first in range(0, taps, many):
-            pieces, used = [], False
-            for tap in range(first, min(first + many, taps)):
-                a, b = tap // BIG - skip, tap % BIG - skip
-                inside = 0 <= a < size and 0 <= b < size
-                used = used or inside
-                pieces.append(raw[a, b] if inside else empty)
-            count = len(pieces) * inner
-            value = (
-                jnp.concatenate(pieces, axis=1) if used else jnp.zeros((channels, count), BF16)
-            )
-            wbig[n * channels : (n + 1) * channels, first * inner : first * inner + count] = value
+    lay3(dec_w, w3d)
+    for a in range(BIG):
+        blocks = []
+        for size, raw in zip(SIZES, raws):
+            skip = PAD - size // 2
+            if skip <= a < skip + size:
+                some = raw[a - skip].reshape(size * inner, channels)
+                edge = [jnp.zeros((skip * inner, channels), BF16)] if skip else []
+                blocks.append(jnp.concatenate(edge + [some] + edge, axis=0))
+            else:
+                blocks.append(jnp.zeros((BIG * inner, channels), BF16))
+        wt[a * BIG * inner : (a + 1) * BIG * inner, :] = jnp.concatenate(blocks, axis=1)
+    taps = BIG * BIG * inner
+    for first in range(0, taps, 128):
+        last = min(first + 128, taps)
+        wbig[:, first:last] = wt[first:last, :].T
 
     total = part[group_of(frame)].astype(F32)
     for step in range(1, frames):
@@ -388,24 +405,31 @@
 ):
     channels, rows, width = features.shape[1:]
     inner = mix_w.shape[0] // GROUPS
+    branches = [jnp.transpose(w, (0, 1, 3, 2)) for w in (branch3, branch5, branch7, branch11)]
     vmem = pl.BlockSpec(memory_space=pltpu.VMEM)
-    hbm = pl.BlockSpec(memory_space=pl.ANY)
+    hbm = pl.BlockSpec(memory_space=pltpu.HBM)
     strip = (rows, channels, width)
     pair = pltpu.SemaphoreType.DMA((2,))
     many = pltpu.SemaphoreType.DMA((frames - 1,))
     decoded = pl.pallas_call(
         functools.partial(kernel, frames, spaces),
         out_shape=jax.ShapeDtypeStruct(strip, BF16),
-        in_specs=[vmem] * 5 + [hbm] * 4 + [vmem] * 3,
+        in_specs=[hbm] * 8 + [vmem] * 4,
         out_specs=vmem,
         scratch_shapes=[
+            pltpu.VMEM((channels, rows, width), BF16),
+            pltpu.VMEM(strip, BF16),
+            pltpu.VMEM(enc_w.shape, BF16),
+            pltpu.VMEM((mix_w.shape[0], 128), BF16),
+            pltpu.VMEM(dec_w.shape, BF16),
+            pltpu.VMEM((BIG * BIG * inner, 4 * channels), BF16),
             pltpu.VMEM((channels, 9 * channels), BF16),
             pltpu.VMEM((channels, 9 * channels), BF16),
             pltpu.VMEM((4 * channels, BIG * BIG * inner), BF16),
-            pltpu.VMEM(branch3.shape, BF16),
-            pltpu.VMEM(branch5.shape, BF16),
-            pltpu.VMEM(branch7.shape, BF16),
-            pltpu.VMEM(branch11.shape, BF16),
+            pltpu.VMEM(branches[0].shape, BF16),
+            pltpu.VMEM(branches[1].shape, BF16),
+            pltpu.VMEM(branches[2].shape, BF16),
+            pltpu.VMEM(branches[3].shape, BF16),
             pltpu.VMEM((rows + 2, 3 * channels, width), BF16),
             pltpu.VMEM((rows + 2 * PAD, BIG * inner, width), BF16),
             pltpu.VMEM(strip, BF16),
@@ -416,7 +440,7 @@
             pltpu.VMEM((2, channels, width), BF16),
             pltpu.VMEM((2, PAD, inner, width), BF16),
             pltpu.VMEM((2, channels, width), BF16),
-            pltpu.SemaphoreType.DMA((4,)),
+            pltpu.SemaphoreType.DMA((8,)),
             pair,
             pair,
             many,
@@ -427,20 +451,17 @@
             pair,
         ],
         compiler_params=pltpu.CompilerParams(
-            collective_id=0, has_side_effects=True, vmem_limit_bytes=40 * 2**20
+            collective_id=0, has_side_effects=True, vmem_limit_bytes=62 * 2**20
         ),
     )(
-        jnp.transpose(features[0], (1, 0, 2)),
+        features,
         enc_w,
+        mix_w,
+        *branches,
+        dec_w,
         enc_b[None],
-        mix_w,
         mix_b[None],
-        branch3,
-        branch5,
-        branch7,
-        branch11,
         branch_b,
-        dec_w,
         dec_b[None],
     )
     return jnp.transpose(decoded, (1, 0, 2))[None]

time: 41.7 us -> 31.9 us (0.76)
  local copies, waits for them, and re-layouts: 12.1 us -> 1.83 us
  Pallas kernels: 29.2 us -> 29.9 us
    unnamed x21 -> x0, local copies, waits for them, and re-layouts: 11.2 us -> none
    broadcast_in_dim x1, local copies, waits for them, and re-layouts: 0.88 us -> 1.83 us  [per_device(): return jnp.transpose(decoded, (1, 0, 2))[None]]
    pallas_call x1, Pallas kernels: 29.2 us -> 29.9 us  [per_device(): pl.pallas_call(functools.partial(kernel, frames, spaces), out_shape=jax.S...]
where the time goes in v2:
time: 31.9 us; the launch traced here: 31.7 us
  Pallas kernels  29.9 us (94%)
  local copies, waits for them, and re-layouts  1.83 us (6%)
    pallas_call x1, Pallas kernels, per_device(): pl.pallas_call(functools.partial(kernel, frames, spaces), out_shape=jax.S...  29.9 us
    broadcast_in_dim x1, local copies, waits for them, and re-layouts, per_device(): return jnp.transpose(decoded, (1, 0, 2))[None]  1.83 us

profile of v2, /device:TPU:13, one launch (start us, length us, event | category | flops | bytes accessed | tf_op | source)
XLA Modules:
  0.0 31.7 jit_solution(12498898721114176486)
XLA Ops:
  0.0 29.9 %shard_map.118 = bf16[16,64,128]{2,1,0:T(8,128)(2,1)} custom-call(bf16[1,64,16,128]{3,2,1,0:T(8,128)(2,1)} %features.1, bf16[3,3,64,64]{3,2,1,0:T(8,128)(2,1)} %enc_w_all.1, bf16[128,512]{1,0:T(8,128)(2,1)} %mix_w.1, bf16[3,3,16,64]{3,2,1,0:T(8,128)(2,1)} %bitcast.14, bf16[5,5,16,64]{3,2,1,0:T(8,128)(2,1)} %bitcast.13, bf16[7,7,16,64]{3,2,1,0:T(8,128)(2,1)} %bitcast.12, ...), custom_call_target="tpu_custom_call" | custom-call | tf_op jit(solution)/shard_map/pallas_call | solution.py:414
  29.9 1.8 %copy.13 = bf16[1,64,16,128]{3,2,1,0:T(8,128)(2,1)} copy(bf16[1,64,16,128]{3,1,2,0:T(8,128)(2,1)} %bitcast.10) | data formatting | bytes 524288 | tf_op jit(solution)/shard_map/broadcast_in_dim | solution.py:467

commit v3 on v2

--- a/solution.py
+++ b/solution.py
@@ -221,52 +221,74 @@
             own_mix,
         )
 
-    pl.semaphore_wait(
-        barrier, frames - 1 + above.astype(jnp.int32) + below.astype(jnp.int32)
-    )
-
-    x_args = (feat.at[0], feat.at[rows - 1], x_halo, x_send, x_recv)
-    edges_start(*x_args)
-
     @pl.loop(0, rows)
     def _(row):
         put3(row + 1, feat[row])
+
+    near = [*range(2, PAD), *range(rows - PAD, rows - 2)]
+    edge = [0, 1, rows - 2, rows - 1]
+    middle = [*range(PAD, rows - PAD)]
+    place = {row: n for n, row in enumerate(near + edge + middle)}
+    chunks = (
+        (0, len(near)),
+        (len(near), len(edge)),
+        (len(near) + len(edge), len(middle)),
+    )
 
     def encode(row):
         e = conv3(w3e, enc_col, row)
         p = jnp.dot(own_mix, e, preferred_element_type=F32).astype(BF16)
         for h in range(2):
             enc[row + h] = e[:, h * width : (h + 1) * width]
-            part[:, row + h] = p[:, h * width : (h + 1) * width].reshape(
+            part[:, place[row + h]] = p[:, h * width : (h + 1) * width].reshape(
                 p.shape[0] // inner, inner, width
             )
 
-    @pl.loop(1, rows // 2 - 1)
-    def _(pair):
-        encode(2 * pair)
+    for row in range(2, rows - 2, 2):
+        encode(row)
+
+    pl.semaphore_wait(
+        barrier, frames - 1 + above.astype(jnp.int32) + below.astype(jnp.int32)
+    )
+
+    x_args = (feat.at[0], feat.at[rows - 1], x_halo, x_send, x_recv)
+    edges_start(*x_args)
+
+    per_group = out_channels // GROUPS
+
+    def group_of(index):
+        return (index * channels) // per_group
+
+    def share(step, chunk):
+        peer = lax.rem(frame + step, frames)
+        first, count = chunks[chunk]
+        flight = chunk * (frames - 1) + step - 1
+        return pltpu.make_async_remote_copy(
+            src_ref=part.at[group_of(peer), first : first + count],
+            dst_ref=arrived.at[step - 1, first : first + count],
+            send_sem=p_send.at[flight],
+            recv_sem=p_recv.at[flight],
+            device_id={"frame": peer},
+            device_id_type=MESH,
+        )
+
+    def summed(chunk):
+        first, count = chunks[chunk]
+        total = part[group_of(frame), first : first + count].astype(F32)
+        for step in range(1, frames):
+            share(step, chunk).wait_recv()
+            total = total + arrived[step - 1, first : first + count].astype(F32)
+        return (total + mix_col[None]).astype(BF16)
+
+    for step in range(1, frames):
+        share(step, 0).start()
 
     edges3(*x_args)
     encode(0)
     encode(rows - 2)
-
-    per_group = out_channels // GROUPS
-
-    def group_of(index):
-        return (index * channels) // per_group
-
-    def share(step):
-        peer = lax.rem(frame + step, frames)
-        return pltpu.make_async_remote_copy(
-            src_ref=part.at[group_of(peer)],
-            dst_ref=arrived.at[step - 1],
-            send_sem=p_send.at[step - 1],
-            recv_sem=p_recv.at[step - 1],
-            device_id={"frame": peer},
-            device_id_type=MESH,
-        )
-
-    for step in range(1, frames):
-        share(step).start()
+    for chunk in (1, 2):
+        for step in range(1, frames):
+            share(step, chunk).start()
 
     dec_col = column(dec_b[...], channels)
     branch_col = jnp.concatenate(
@@ -292,13 +314,11 @@
         last = min(first + 128, taps)
         wbig[:, first:last] = wt[first:last, :].T
 
-    total = part[group_of(frame)].astype(F32)
-    for step in range(1, frames):
-        share(step).wait_recv()
-        total = total + arrived[step - 1].astype(F32)
-    total = (total + mix_col[None]).astype(BF16)
-    hid[...] = total
-    h_args = (hid.at[0:PAD], hid.at[rows - PAD : rows], h_halo, h_send, h_recv)
+    some, outer = summed(0), summed(1)
+    half = len(near) // 2
+    hid[0] = jnp.concatenate([outer[:2], some[:half]], axis=0)
+    hid[1] = jnp.concatenate([some[half:], outer[2:]], axis=0)
+    h_args = (hid.at[0], hid.at[1], h_halo, h_send, h_recv)
     edges_start(*h_args)
 
     def put11(row, x):
@@ -309,7 +329,9 @@
                 shifted(x, tap - PAD).astype(BF16).reshape(count, inner, width)
             )
 
-    put11(PAD, total)
+    put11(PAD, hid[0])
+    put11(rows, hid[1])
+    put11(2 * PAD, summed(2))
 
     def mixed(row):
         depth = BIG * BIG * inner
@@ -325,13 +347,6 @@
             joined[row + h] = whole
             put3(row + h + 1, whole)
 
-    low = (PAD + 1) // 2
-    high = (rows - PAD) // 2
-
-    @pl.loop(low, high)
-    def _(pair):
-        mixed(2 * pair)
-
     nothing = jnp.zeros((PAD, BIG * inner, width), BF16)
 
     @pl.when(above)
@@ -359,11 +374,7 @@
     j_args = (joined.at[0], joined.at[rows - 1], j_halo, j_send, j_recv)
     edges_start(*j_args)
 
-    @pl.loop(1, low)
-    def _(pair):
-        mixed(2 * pair)
-
-    @pl.loop(high, rows // 2 - 1)
+    @pl.loop(1, rows // 2 - 1)
     def _(pair):
         mixed(2 * pair)
 
@@ -383,8 +394,9 @@
     edges_sent(*x_args)
     edges_sent(*h_args)
     edges_sent(*j_args)
-    for step in range(1, frames):
-        share(step).wait_send()
+    for chunk in range(len(chunks)):
+        for step in range(1, frames):
+            share(step, chunk).wait_send()
 
 
 def per_device(
@@ -410,10 +422,10 @@
     hbm = pl.BlockSpec(memory_space=pltpu.HBM)
     strip = (rows, channels, width)
     pair = pltpu.SemaphoreType.DMA((2,))
-    many = pltpu.SemaphoreType.DMA((frames - 1,))
+    many = pltpu.SemaphoreType.DMA((3 * (frames - 1),))
     decoded = pl.pallas_call(
         functools.partial(kernel, frames, spaces),
-        out_shape=jax.ShapeDtypeStruct(strip, BF16),
+        out_shape=pltpu.VMEM(strip, BF16),
         in_specs=[hbm] * 8 + [vmem] * 4,
         out_specs=vmem,
         scratch_shapes=[
@@ -435,7 +447,7 @@
             pltpu.VMEM(strip, BF16),
             pltpu.VMEM((GROUPS, rows, inner, width), BF16),
             pltpu.VMEM((frames - 1, rows, inner, width), BF16),
-            pltpu.VMEM((rows, inner, width), BF16),
+            pltpu.VMEM((2, PAD, inner, width), BF16),
             pltpu.VMEM(strip, BF16),
             pltpu.VMEM((2, channels, width), BF16),
             pltpu.VMEM((2, PAD, inner, width), BF16),

time: 31.9 us -> 29.4 us (0.922)
  the two profiles are of different devices: /device:TPU:13 before, /device:TPU:1 now
where the time goes in v3:
time: 29.4 us; the launch traced here: 29.2 us
  Pallas kernels  28.3 us (96%)
  local copies, waits for them, and re-layouts  0.88 us (3%)
    pallas_call x1, Pallas kernels, per_device(): pl.pallas_call(functools.partial(kernel, frames, spaces), out_shape=pltpu...  28.3 us
    broadcast_in_dim x1, local copies, waits for them, and re-layouts, per_device(): return jnp.transpose(decoded, (1, 0, 2))[None]  0.88 us

profile of v3, /device:TPU:1, one launch (start us, length us, event | category | flops | bytes accessed | tf_op | source)
XLA Modules:
  0.0 29.2 jit_solution(15389638952365134482)
XLA Ops:
  0.0 28.3 %shard_map.118 = bf16[16,64,128]{2,1,0:T(8,128)(2,1)S(1)} custom-call(bf16[1,64,16,128]{3,2,1,0:T(8,128)(2,1)} %features.1, bf16[3,3,64,64]{3,2,1,0:T(8,128)(2,1)} %enc_w_all.1, bf16[128,512]{1,0:T(8,128)(2,1)} %mix_w.1, bf16[3,3,16,64]{3,2,1,0:T(8,128)(2,1)} %bitcast.14, bf16[5,5,16,64]{3,2,1,0:T(8,128)(2,1)} %bitcast.13, bf16[7,7,16,64]{3,2,1,0:T(8,128)(2,1)} %bitcast.12, ...), custom_call_target="tpu_custom_call" | custom-call | tf_op jit(solution)/shard_map/pallas_call | solution.py:426
  28.3 0.9 %copy.13 = bf16[1,64,16,128]{3,2,1,0:T(8,128)(2,1)} copy(bf16[1,64,16,128]{3,1,2,0:T(8,128)(2,1)S(1)} %bitcast.10) | data formatting | bytes 524288 | tf_op jit(solution)/shard_map/broadcast_in_dim | solution.py:479
